TPU v7x, 32 devices: a whole 2x2x4 slice. The times are simulated.
32 devices in a mesh: parts: 2 (over y), slab: 4 (over z), ang: 2 (over x), chan: 2 (over core).
Axes of the slice: x: 2, y: 2, z: 4, core: 2. Of those that a mesh axis runs over, the one named last changes fastest.
Arguments:
- sinogram: bfloat16 [4, 2, 512, 1024], P(('parts', 'chan'), 'ang', 'slab'), parts along dimension 0, may hold values from -6 to 6
- transaxial: bfloat16 [2, 1024, 1024], P('ang', 'slab'), may hold values from -0.1875 to 0.1875
- targets: int32 [2, 64, 1], P('ang'), may hold values from 0 to 3; in each aligned block of 16 rows (0 to 15, 16 to 31, ..., all dimensions but the last counted through in order) at most 8 rows name the same one
- row_shift: float32 [2, 64], P('ang'), may hold values from -2 to 2
- center: float32 [2, 4096], P('ang', 'slab'), may hold values from 0 to 8
- spread: float32 [2, 4096], P('ang', 'slab'), may hold values from 0.5 to 4
- gain: float32 [2, 4096], P('ang', 'slab'), may hold values from 0.1 to 0.4
Outputs:
- volume: float32 [4, 1024, 4096], P(('parts', 'chan'), 'ang', 'slab'), parts along dimension 0
There are 2 independent parts, one for each index of `parts`. A program takes and returns all parts, laid end to end along the dimension named above; an argument that names none is the same for every part. Nothing has to cross between parts.
Inputs may be any that keep to these rules, and one draw needn't show every extreme that they name: `targets`: within one angle, the 16 sub-blocks of one slab device name any one slab at most 8 times, a bound that some block reaches.
All inputs are finite; a program needn't handle non-finite values.
Results may differ from a plain program's by a relative error of at most 0.015.
Values may be sent and summed in bfloat16 or wider, within the bound.
A program may use at most 64 MiB of HBM per device.

v0:
```python
import jax
import jax.numpy as jnp
from jax import lax
from jax.sharding import PartitionSpec as P


def footprint_tile(local_pos, row_center, row_spread, row_gain, live):
    offset = (local_pos[None, :] - row_center[:, None]) / row_spread[:, None]
    tile = row_gain[:, None] * lax.rsqrt(row_spread)[:, None] / (1.0 + offset * offset)
    return jnp.where(live[None, :], tile, 0.0).astype(jnp.bfloat16)


def shards(sinogram, transaxial, targets, row_shift, center, spread, gain):
    slab_count = lax.axis_size("slab")
    my_slab = lax.axis_index("slab")
    detector = sinogram[0, 0]
    block_rows = detector.shape[0]
    table_flat = targets[0, :, 0]
    shift_flat = row_shift[0]
    sub_total = table_flat.shape[0]
    subs_count = sub_total // slab_count
    sub_rows = block_rows // subs_count
    capacity = max(2, 2 * subs_count // slab_count)
    row_center = center[0]
    row_spread = spread[0]
    row_gain = gain[0]
    weights_full = lax.all_gather(transaxial[0], "slab", axis=0, tiled=True)
    slot_rows = capacity * sub_rows
    piece = lax.all_gather(detector, "slab", axis=0, tiled=True)
    count = piece.shape[0]
    spanned = -(-count // block_rows) + 1
    slot_count = min(count, spanned * slot_rows)
    coords_int = jnp.arange(count, dtype=jnp.int32)
    sub_index = coords_int // sub_rows
    hit = sub_index[:, None] == jnp.arange(sub_total, dtype=jnp.int32)[None, :]
    picked = jnp.sum(jnp.where(hit, table_flat[None, :], 0), axis=1)
    shifted = jnp.sum(jnp.where(hit, shift_flat[None, :], 0.0), axis=1)
    live = picked == my_slab
    live_order = jnp.cumsum(live.astype(jnp.int32)) - 1
    select = live[None, :] & (
        live_order[None, :] == jnp.arange(slot_count, dtype=jnp.int32)[:, None]
    )
    chosen = jnp.dot(select.astype(jnp.bfloat16), piece, preferred_element_type=jnp.float32).astype(
        jnp.bfloat16
    )
    slot_coord = jnp.sum(jnp.where(select, coords_int[None, :], 0), axis=1)
    slot_shift = jnp.sum(jnp.where(select, shifted[None, :], 0.0), axis=1)
    slot_live = jnp.any(select, axis=1)
    local_pos = (slot_coord % sub_rows).astype(jnp.float32) + 0.5 - slot_shift
    tile = footprint_tile(local_pos, row_center, row_spread, row_gain, slot_live)
    axial = jnp.dot(tile, chosen, preferred_element_type=jnp.float32)
    axial_half = axial.astype(jnp.bfloat16)
    piece = weights_full
    volume = lax.psum_scatter(
        lax.dot_general(
            piece, axial_half, (((1,), (1,)), ((), ())), preferred_element_type=jnp.float32
        ).astype(jnp.bfloat16),
        "ang",
        scatter_dimension=0,
        tiled=True,
    ).astype(jnp.float32)
    return volume[None]


def solution(mesh):
    in_specs = (
        P(("parts", "chan"), "ang", "slab", None),
        P("ang", "slab", None),
        P("ang", None, None),
        P("ang", None),
        P("ang", "slab"),
        P("ang", "slab"),
        P("ang", "slab"),
    )
    out_specs = P(("parts", "chan"), "ang", "slab")
    return jax.shard_map(shards, mesh=mesh, in_specs=in_specs, out_specs=out_specs, check_vma=False)
```

profile of v0, /device:TPU:0, one launch (start us, length us, event | category | flops | bytes accessed | tf_op | source)
XLA Modules:
  0.0 133.9 jit_solution(12672904034560360003)
XLA Ops:
  6.5 0.0 all-gather.5.cloned.1.call-start
  6.5 0.7 all-gather.5.cloned.1.call-update
  7.3 0.0 all-gather.7.cloned.1.call-start
  7.3 0.7 all-gather.7.cloned.1.call-update
  8.0 0.0 reduce-scatter.2.cloned.1.call-start
  8.1 0.8 select_reduce_fusion.3
  8.8 0.3 reduce-window.9
  9.1 0.1 slice.7
  9.3 0.1 slice_reduce_fusion
  9.4 0.8 select_reduce_fusion.2
  10.1 0.1 add_bitcast_fusion
  10.2 0.2 fusion.26
  10.4 0.2 select_reduce_fusion.1
  10.6 0.2 select_reduce_fusion
  10.9 0.7 rsqrt_multiply_fusion
  11.6 28.0 %all-gather.5.cloned.1.call-done = bf16[1,1,512,1024]{3,2,1,0:T(8,128)(2,1)} async-done(((bf16[1,1,128,1024]{3,2,1,0:T(8,128)(2,1)}), bf16[1,1,512,1024]{3,2,1,0:T(8,128)(2,1)}) %all-gather.5.cloned.1.call-update) | async-done | bytes 1048592 | tf_op jit(solution)/shard_map/all_gather | solution.py:29
  39.6 1.7 %convolution_convert_fusion = bf16[320,1024]{1,0:T(8,128)(2,1)S(1)} fusion(bf16[1,1,512,1024]{3,2,1,0:T(8,128)(2,1)} %all-gather.5.cloned.1.call-done, s32[512]{0:T(512)S(1)} %add_bitcast_fusion, pred[512]{0:T(512)(128)(4,1)S(1)} %get-tuple-element.6), kind=kOutput, calls=%fused_computation.6 | convolution fusion | flops 336199680 | bytes 1706496 | tf_op jit(solution)/shard_map/dot_general | solution.py:43
  41.3 45.3 %all-gather.7.cloned.1.call-done = bf16[1,1024,1024]{2,1,0:T(8,128)(2,1)} async-done(((bf16[1,256,1024]{2,1,0:T(8,128)(2,1)}), bf16[1,1024,1024]{2,1,0:T(8,128)(2,1)}) %all-gather.7.cloned.1.call-update) | async-done | bytes 2097168 | tf_op jit(solution)/shard_map/all_gather | solution.py:27
  86.6 0.0 copy-done
  86.6 6.7 %convert_bitcast_fusion = bf16[1024,1024]{0,1:T(8,128)(2,1)} fusion(bf16[1,1024,1024]{2,1,0:T(8,128)(2,1)} %all-gather.7.cloned.1.call-done, bf16[320,1024]{1,0:T(8,128)(2,1)S(1)} %convolution_convert_fusion, f32[1024]{0:T(1024)S(1)} %bitcast.25, f32[1024]{0:T(1024)S(1)} %bitcast.28, f32[320]{0:T(512)S(1)} %fusion.32, f32[1024]{0:T(1024)S(1)} %rsqrt_multiply_fusion, ...), kind=kOutput, calls=%fused_computation.2 | convolution fusion | flops 2822963200 | bytes 4863552 | tf_op jit(solution)/shard_map/dot_general | solution.py:55
  93.3 0.0 reduce-scatter.2.cloned.1.call-update
  93.3 30.7 %reduce-scatter.2.cloned.1.call-done = bf16[512,1024]{0,1:T(8,128)(2,1)} async-done(((bf16[1024,1024]{0,1:T(8,128)(2,1)}), bf16[512,1024]{0,1:T(8,128)(2,1)}) %reduce-scatter.2.cloned.1.call-update) | async-done | bytes 1048592 | tf_op jit(solution)/shard_map/reduce_scatter | solution.py:54
  124.0 1.5 %bitcast_convert_fusion = f32[1,512,1024]{1,2,0:T(8,128)S(1)} fusion(bf16[512,1024]{0,1:T(8,128)(2,1)} %reduce-scatter.2.cloned.1.call-done), kind=kLoop, calls=%fused_computation.7 | loop fusion | flops 524288 | bytes 3145728 | tf_op jit(solution)/shard_map/broadcast_in_dim | solution.py:62
  125.5 1.8 %copy.10 = f32[1,512,1024]{2,1,0:T(8,128)} copy(f32[1,512,1024]{1,2,0:T(8,128)S(1)} %bitcast_convert_fusion) | data formatting | bytes 4194304 | tf_op jit(solution)/shard_map/broadcast_in_dim | solution.py:62
  (7 shorter events, 0.1 us)
Async XLA Ops:
  6.5 80.1 %copy-start = (f32[1,1024]{1,0:T(1,128)S(1)}, f32[1,1024]{1,0:T(1,128)}, u32[]{:S(2)}) copy-start(f32[1,1024]{1,0:T(1,128)} %param.12) | copy-start | bytes 12292
  6.5 80.1 %copy-start.1 = (f32[1,1024]{1,0:T(1,128)S(1)}, f32[1,1024]{1,0:T(1,128)}, u32[]{:S(2)}) copy-start(f32[1,1024]{1,0:T(1,128)} %param.11) | copy-start | bytes 12292
  6.5 33.1 %all-gather.5.cloned.1.call-start = ((), (), s32[]{:S(2)}) async-start(), calls=%async_computation.2 | async-start | bytes 1310720 | tf_op jit(solution)/shard_map/all_gather | solution.py:29
  7.3 79.4 %all-gather.7.cloned.1.call-start = ((), (), s32[]{:S(2)}) async-start(), calls=%async_computation.3 | async-start | bytes 2621440 | tf_op jit(solution)/shard_map/all_gather | solution.py:27
  8.0 116.0 %reduce-scatter.2.cloned.1.call-start = ((), (), s32[]{:S(2)}) async-start(), calls=%async_computation.1 | async-start | bytes 3145728 | tf_op jit(solution)/shard_map/reduce_scatter | solution.py:54
Sparse Core Ops, SparseCore 0:
  8.9 30.6 all-gather.4
  41.2 45.4 all-gather.6
  93.5 30.5 reduce-scatter.1
where the time goes:
time: 134 us
  waiting for transfers between devices  105 us (78%)
  between operations  13.1 us (10%)
  matrix products  8.42 us (6%)
  other arithmetic  4.81 us (4%)
  local copies, waits for them, and re-layouts  2.01 us (1%)
    all_gather x1, waiting for transfers between devices, shards(): weights_full = lax.all_gather(transaxial[0], 'slab', axis=0, tiled=True)  45.3 us
    reduce_scatter x1, waiting for transfers between devices, shards(): lax.psum_scatter(lax.dot_general(piece, axial_half, (((1,), (1,)), ((), (...  30.7 us
    all_gather x1, waiting for transfers between devices, shards(): piece = lax.all_gather(detector, 'slab', axis=0, tiled=True)  28 us
    dot_general x1, matrix products, shards(): lax.dot_general(piece, axial_half, (((1,), (1,)), ((), ())), preferred_el...  6.69 us
  transfers between devices with their start and end apart: 3, of which 3 were waited for; matrix products, arithmetic and copies ran while one was open for 4% of the time, Pallas kernels for 0%

commit v1 on v0

v1 whole, which is shorter than its diff:
```python
import functools

import jax
import jax.numpy as jnp
from jax import lax
from jax.experimental import pallas as pl
from jax.experimental.pallas import tpu as pltpu
from jax.sharding import PartitionSpec as P

MESH = pl.DeviceIdType.MESH
F32 = jnp.float32
BF16 = jnp.bfloat16


def log2(n):
    assert n & (n - 1) == 0
    return n.bit_length() - 1


def iota(shape, dim):
    return lax.broadcasted_iota(jnp.int32, shape, dim)


def keep(mask, value):
    return jnp.where(mask, value, jnp.zeros_like(value))


def kernel(
    nz, na, subs, cap,
    x_ref, w_ref, targets_ref, shift_ref, center_ref, spread_ref, gain_ref,
    g_out, tile_out,
    w_full, send_rows, rows, g_send, g_recv, meta, pos,
    own_sem, row_ss, row_rs, up_ss, down_ss, wz_rs, wy_ss, wy_rs, wc_ss, wc_rs,
    wd_ss, wd_rs, meta_ss, meta_rs, g_ss, g_rs,
):
    p = lax.axis_index("parts")
    z = lax.axis_index("slab")
    a = lax.axis_index("ang")
    c = lax.axis_index("chan")
    v_rows, width = x_ref.shape
    x_block = w_ref.shape[0]
    quarter = x_block // 4
    sub_rows = v_rows // subs
    total = nz * subs
    piece = cap * sub_rows
    slots = nz * piece
    x_part = g_out.shape[0]
    l_sub, l_subs, l_piece = log2(sub_rows), log2(subs), log2(piece)

    barrier = pltpu.get_barrier_semaphore()
    for d in range(1, nz):
        pl.semaphore_signal(
            barrier, inc=1, device_id={"slab": lax.rem(z + d, nz)}, device_id_type=MESH
        )
    for d in range(1, na):
        pl.semaphore_signal(
            barrier, inc=1, device_id={"ang": lax.rem(a + d, na)}, device_id_type=MESH
        )
    pl.semaphore_signal(barrier, inc=1, device_id={"parts": 1 - p}, device_id_type=MESH)
    pl.semaphore_signal(barrier, inc=1, device_id={"chan": 1 - c}, device_id_type=MESH)

    t_col = targets_ref[...].astype(F32)
    eye = iota((total, total), 0) == iota((total, total), 1)
    t_row = jnp.sum(keep(eye, jnp.broadcast_to(t_col, (total, total))), axis=0, keepdims=True)
    meta[a, 0:1, :] = center_ref[...]
    meta[a, 1:2, :] = spread_ref[...]
    meta[a, 2:3, :] = gain_ref[...]
    meta[a, 3:4, 0:total] = t_row
    meta[a, 4:5, 0:total] = shift_ref[...]

    b_of_v = z * subs + (iota((total, v_rows), 1) >> l_sub)
    b_col = iota((total, v_rows), 0)
    t_wide = jnp.broadcast_to(t_col, (total, v_rows))
    t_v = jnp.sum(keep(b_col == b_of_v, t_wide), axis=0, keepdims=True)
    before = (t_wide == t_v) & (b_col >= z * subs) & (b_col < b_of_v)
    rank_v = jnp.sum(before.astype(F32), axis=0, keepdims=True)
    slot = iota((slots, v_rows), 0)
    v_id = iota((slots, v_rows), 1)
    pick = (
        (t_v == (slot >> l_piece).astype(F32))
        & (rank_v == ((slot & (piece - 1)) >> l_sub).astype(F32))
        & ((v_id & (sub_rows - 1)) == (slot & (sub_rows - 1)))
    )
    send_rows[...] = jnp.dot(
        pick.astype(F32).astype(BF16), x_ref[...], preferred_element_type=F32
    ).astype(BF16)

    pl.semaphore_wait(barrier, nz - 1 + na - 1 + 2)

    def weight_slice(s, qp, qc):
        start = pl.multiple_of(s * x_block + (qp * 2 + qc) * quarter, quarter)
        return w_full.at[pl.ds(start, quarter)]

    def weight_copy(s, qp, qc, ss, rs, device, src=None):
        block = weight_slice(s, qp, qc)
        return pltpu.make_async_remote_copy(
            src_ref=block if src is None else src, dst_ref=block,
            send_sem=ss.at[s], recv_sem=rs.at[s], device_id=device, device_id_type=MESH,
        )

    def up(s, src=None):
        return weight_copy(s, p, c, up_ss, wz_rs, {"slab": lax.rem(z + 1, nz)}, src)

    def down(s, src=None):
        return weight_copy(s, p, c, down_ss, wz_rs, {"slab": lax.rem(z + nz - 1, nz)}, src)

    def across(s, qp=p):
        return weight_copy(s, qp, c, wy_ss, wy_rs, {"parts": 1 - p})

    def twin(s, qc=c):
        return weight_copy(s, p, qc, wc_ss, wc_rs, {"chan": 1 - c})

    def twin_far(s, qc=c):
        return weight_copy(s, 1 - p, qc, wd_ss, wd_rs, {"chan": 1 - c})

    own_quarter = w_ref.at[pl.ds(pl.multiple_of((p * 2 + c) * quarter, quarter), quarter)]

    @pl.when(z + 1 < nz)
    def _():
        up(z, own_quarter).start()

    @pl.when(z > 0)
    def _():
        down(z, own_quarter).start()

    def row_copy(src_z, dst_z):
        return pltpu.make_async_remote_copy(
            src_ref=send_rows.at[pl.ds(pl.multiple_of(dst_z * piece, piece), piece)],
            dst_ref=rows.at[pl.ds(pl.multiple_of(src_z * piece, piece), piece)],
            send_sem=row_ss.at[dst_z], recv_sem=row_rs.at[src_z],
            device_id={"slab": dst_z}, device_id_type=MESH,
        )

    for d in range(1, nz):
        row_copy(z, lax.rem(z + d, nz)).start()

    def meta_copy(src_a, dst_a):
        return pltpu.make_async_remote_copy(
            src_ref=meta.at[src_a], dst_ref=meta.at[src_a],
            send_sem=meta_ss.at[dst_a], recv_sem=meta_rs.at[src_a],
            device_id={"ang": dst_a}, device_id_type=MESH,
        )

    for d in range(1, na):
        meta_copy(a, lax.rem(a + d, na)).start()

    own_copy = pltpu.make_async_copy(
        w_ref, w_full.at[pl.ds(pl.multiple_of(z * x_block, x_block), x_block)], own_sem
    )
    own_copy.start()
    mine = pl.ds(pl.multiple_of(z * piece, piece), piece)
    rows[mine, :] = send_rows[mine, :]

    def make_tile(src_a):
        t_r = meta[src_a, 3:4, 0:total]
        s_r = meta[src_a, 4:5, 0:total]
        t_c = jnp.sum(keep(eye, jnp.broadcast_to(t_r, (total, total))), axis=1, keepdims=True)
        b0, b1 = iota((total, total), 0), iota((total, total), 1)
        earlier = (t_c == t_r) & ((b0 >> l_subs) == (b1 >> l_subs)) & (b0 < b1)
        rank = jnp.sum(earlier.astype(F32), axis=0, keepdims=True)
        sl = iota((slots, total), 0)
        b = iota((slots, total), 1)
        match = (
            ((b >> l_subs) == (sl >> l_piece))
            & (t_r == z.astype(F32))
            & (rank == ((sl & (piece - 1)) >> l_sub).astype(F32))
        )
        shift = jnp.sum(keep(match, jnp.broadcast_to(s_r, (slots, total))), axis=1, keepdims=True)
        j = (iota((slots, 1), 0) & (sub_rows - 1)).astype(F32)
        pos[...] = j + 0.5 - shift
        center = meta[src_a, 0:1, :]
        spread = meta[src_a, 1:2, :]
        scale = meta[src_a, 2:3, :] * lax.rsqrt(spread)
        inverse = 1.0 / spread
        step = min(32, slots)

        @pl.loop(0, slots // step)
        def _(i):
            at = pl.multiple_of(i * step, step)
            offset = (pos[pl.ds(at, step), :] - center) * inverse
            tile_out[pl.ds(pl.multiple_of(src_a * slots + at, step), step), :] = (
                scale / (1.0 + offset * offset)
            ).astype(BF16)

    make_tile(a)

    for t in range(1, nz):
        below, above = z - t, z + t

        @pl.when(below >= 0)
        def _():
            up(below).wait_recv()

            @pl.when(z + 1 < nz)
            def _():
                up(below).start()

            across(below).start()
            twin(below).start()

        @pl.when(above < nz)
        def _():
            down(above).wait_recv()

            @pl.when(z > 0)
            def _():
                down(above).start()

            across(above).start()
            twin(above).start()

        for s, there in ((below, below >= 0), (above, above < nz)):
            @pl.when(there)
            def _():
                across(s, 1 - p).wait_recv()
                twin_far(s).start()

    for d in range(1, na):
        src_a = lax.rem(a + d, na)
        meta_copy(src_a, a).wait_recv()
        make_tile(src_a)

    for d in range(1, nz):
        row_copy(lax.rem(z + d, nz), z).wait_recv()
    own_copy.wait()
    for d in range(1, nz):
        s = lax.rem(z + d, nz)
        twin(s, 1 - c).wait_recv()
        twin_far(s, 1 - c).wait_recv()

    def g_copy(src_a, dst_a):
        return pltpu.make_async_remote_copy(
            src_ref=g_send.at[dst_a], dst_ref=g_recv.at[src_a],
            send_sem=g_ss.at[dst_a], recv_sem=g_rs.at[src_a],
            device_id={"ang": dst_a}, device_id_type=MESH,
        )

    x_tile = min(256, x_part)

    def project(dst_a, out):
        @pl.loop(0, x_part // x_tile)
        def _(i):
            at = pl.multiple_of(i * x_tile, x_tile)
            block = w_full[pl.ds(pl.multiple_of(dst_a * x_part + at, x_tile), x_tile), :]
            out[pl.ds(at, x_tile), :] = lax.dot_general(
                block, rows[...], (((1,), (1,)), ((), ())), preferred_element_type=F32
            ).astype(BF16)

    for d in range(1, na):
        dst_a = lax.rem(a + d, na)
        project(dst_a, g_send.at[dst_a])
        g_copy(a, dst_a).start()
    project(a, g_recv.at[a])

    for d in range(1, na):
        g_copy(lax.rem(a + d, na), a).wait_recv()
    for k in range(na):
        g_out[:, k * slots:(k + 1) * slots] = g_recv[k]

    for d in range(1, nz):
        row_copy(z, lax.rem(z + d, nz)).wait_send()
    for d in range(1, na):
        meta_copy(a, lax.rem(a + d, na)).wait_send()
        g_copy(a, lax.rem(a + d, na)).wait_send()
    for s in range(nz):
        @pl.when((s <= z) & (z + 1 < nz))
        def _():
            up(s).wait_send()

        @pl.when((s >= z) & (z > 0))
        def _():
            down(s).wait_send()

        @pl.when(s != z)
        def _():
            across(s).wait_send()
            twin(s).wait_send()
            twin_far(s).wait_send()


def shards(sinogram, transaxial, targets, row_shift, center, spread, gain):
    nz = lax.axis_size("slab")
    na = lax.axis_size("ang")
    detector = sinogram[0, 0]
    weights = transaxial[0]
    v_rows, width = detector.shape
    total = targets.shape[1]
    subs = total // nz
    sub_rows = v_rows // subs
    cap = max(2, 2 * subs // nz)
    piece = cap * sub_rows
    slots = nz * piece
    x_all = weights.shape[0] * nz
    x_part = x_all // na
    r_rows = center.shape[1]
    vmem = pl.BlockSpec(memory_space=pltpu.VMEM)
    dma = pltpu.SemaphoreType.DMA
    projected, tile = pl.pallas_call(
        functools.partial(kernel, nz, na, subs, cap),
        out_shape=(
            jax.ShapeDtypeStruct((x_part, na * slots), BF16),
            jax.ShapeDtypeStruct((na * slots, r_rows), BF16),
        ),
        in_specs=[vmem, pl.BlockSpec(memory_space=pl.ANY)] + [vmem] * 5,
        out_specs=(vmem, vmem),
        scratch_shapes=[
            pltpu.VMEM((x_all, width), BF16),
            pltpu.VMEM((slots, width), BF16),
            pltpu.VMEM((slots, width), BF16),
            pltpu.VMEM((na, x_part, slots), BF16),
            pltpu.VMEM((na, x_part, slots), BF16),
            pltpu.VMEM((na, 8, r_rows), F32),
            pltpu.VMEM((slots, 1), F32),
            dma(()),
        ] + [dma((nz,))] * 11 + [dma((na,))] * 4,
        compiler_params=pltpu.CompilerParams(
            collective_id=0, has_side_effects=True, vmem_limit_bytes=32 * 1024 * 1024
        ),
    )(detector, weights, targets[0], row_shift, center, spread, gain)
    volume = jnp.dot(projected, tile, preferred_element_type=F32)
    return volume[None]


def solution(mesh):
    assert mesh.shape["parts"] == 2 and mesh.shape["chan"] == 2
    in_specs = (
        P(("parts", "chan"), "ang", "slab", None),
        P("ang", "slab", None),
        P("ang", None, None),
        P("ang", None),
        P("ang", "slab"),
        P("ang", "slab"),
        P("ang", "slab"),
    )
    out_specs = P(("parts", "chan"), "ang", "slab")
    return jax.shard_map(shards, mesh=mesh, in_specs=in_specs, out_specs=out_specs, check_vma=False)
```

time: 134 us -> 49.2 us (0.37)
  waiting for transfers between devices: 105 us -> 0 us
  Pallas kernels: 0 us -> 41.4 us
  between operations: 13.1 us -> 0.02 us
  matrix products: 8.42 us -> 2.03 us
  other arithmetic: 4.81 us -> 0 us
  local copies, waits for them, and re-layouts: 2.01 us -> 5.45 us
    all_gather x2 -> x0, waiting for transfers between devices: 73.3 us -> none  [the longest x1 45.3 us: shards(): weights_full = lax.all_gather(transaxial[0], 'slab', axis=0, tiled=True)]
    pallas_call x0 -> x1, Pallas kernels: none -> 41.4 us  [shards(): pl.pallas_call(functools.partial(kernel, nz, na, subs, cap), out_shape=(j...]
    reduce_scatter x1 -> x0, waiting for transfers between devices: 30.7 us -> none  [shards(): lax.psum_scatter(lax.dot_general(piece, axial_half, (((1,), (1,)), ((), (...]
    dot_general x2 -> x1, matrix products: 8.42 us -> 2.03 us  [shards(): volume = jnp.dot(projected, tile, preferred_element_type=F32)]
    unnamed x4 -> x12, local copies, waits for them, and re-layouts: 0.01 us -> 4.7 us
    reduce_sum x4 -> x0, other arithmetic: 1.96 us -> none  [the longest x1 0.75 us: shards(): shifted = jnp.sum(jnp.where(hit, shift_flat[None, :], 0.0), axis=1)]
    broadcast_in_dim x1 -> x0, local copies, waits for them, and re-layouts: 1.81 us -> none  [shards(): return volume[None]]
    broadcast_in_dim x1 -> x0, other arithmetic: 1.5 us -> none  [shards(): return volume[None]]
  transfers between devices with their start and end apart: 3 -> 0, of which waited for: 3 -> 0; matrix products, arithmetic and copies ran while one was open for 4% -> 0% of each run, Pallas kernels for 0% -> 0%
where the time goes in v1:
time: 49.2 us; the launch traced here: 48.9 us
  Pallas kernels  41.4 us (84%)
  local copies, waits for them, and re-layouts  5.45 us (11%)
  matrix products  2.03 us (4%)
    pallas_call x1, Pallas kernels, shards(): pl.pallas_call(functools.partial(kernel, nz, na, subs, cap), out_shape=(j...  41.4 us
    unnamed x12, local copies, waits for them, and re-layouts  4.7 us
    dot_general x1, matrix products, shards(): volume = jnp.dot(projected, tile, preferred_element_type=F32)  2.03 us

profile of v1, /device:TPU:0, one launch (start us, length us, event | category | flops | bytes accessed | tf_op | source)
XLA Modules:
  0.0 48.9 jit_solution(4815934645061100577)
XLA Ops:
  0.0 0.7 %copy.8.targets_ref = s32[64,1]{1,0:T(8,128)S(1)} copy(s32[64,1]{0,1:T(1,128)} %bitcast.9) | data formatting | bytes 512 | tf_op jit(solution)/shard_map/squeeze | solution.py:319
  0.7 0.0 copy-start
  0.7 1.0 %copy-done = bf16[1,256,1024]{2,1,0:T(8,128)(2,1)S(1)} copy-done((bf16[1,256,1024]{2,1,0:T(8,128)(2,1)S(1)}, bf16[1,256,1024]{2,1,0:T(8,128)(2,1)}, u32[]{:S(2)}) %copy-start) | copy-done | bytes 524312
  1.8 0.0 copy-start.1
  1.8 0.9 %copy-done.1 = bf16[1,1,128,1024]{3,2,1,0:T(8,128)(2,1)S(1)} copy-done((bf16[1,1,128,1024]{3,2,1,0:T(8,128)(2,1)S(1)}, bf16[1,1,128,1024]{3,2,1,0:T(8,128)(2,1)}, u32[]{:S(2)}) %copy-start.1) | copy-done | bytes 262168
  2.7 0.0 copy-start.2
  2.7 0.7 %copy-done.2 = f32[1,1024]{1,0:T(1,128)S(1)} copy-done((f32[1,1024]{1,0:T(1,128)S(1)}, f32[1,1024]{1,0:T(1,128)}, u32[]{:S(2)}) %copy-start.2) | copy-done | bytes 4120
  3.4 0.0 copy-start.3
  3.4 0.7 %copy-done.3 = f32[1,1024]{1,0:T(1,128)S(1)} copy-done((f32[1,1024]{1,0:T(1,128)S(1)}, f32[1,1024]{1,0:T(1,128)}, u32[]{:S(2)}) %copy-start.3) | copy-done | bytes 4120
  4.1 0.0 copy-start.4
  4.1 0.7 %copy-done.4 = f32[1,1024]{1,0:T(1,128)S(1)} copy-done((f32[1,1024]{1,0:T(1,128)S(1)}, f32[1,1024]{1,0:T(1,128)}, u32[]{:S(2)}) %copy-start.4) | copy-done | bytes 4120
  4.8 0.0 copy-start.5
  4.8 0.7 %copy-done.5 = f32[1,64]{1,0:T(1,128)S(1)} copy-done((f32[1,64]{1,0:T(1,128)S(1)}, f32[1,64]{1,0:T(1,128)}, u32[]{:S(2)}) %copy-start.5) | copy-done | bytes 280
  5.5 41.4 %shard_map.73 = (bf16[512,512]{1,0:T(8,128)(2,1)S(1)}, bf16[512,1024]{1,0:T(8,128)(2,1)S(1)}) custom-call(bf16[128,1024]{1,0:T(8,128)(2,1)S(1)} %bitcast.8, bf16[256,1024]{1,0:T(8,128)(2,1)S(1)} %bitcast.7, s32[64,1]{1,0:T(8,128)S(1)} %copy.8.targets_ref, f32[1,64]{1,0:T(1,128)S(1)} %copy-done.5, f32[1,1024]{1,0:T(1,128)S(1)} %copy-done.2, ...), custom_call_target="tpu_custom_call" | custom-call | tf_op jit(solution)/shard_map/pallas_call | solution.py:298
  46.8 2.0 %convolution_bitcast_fusion = f32[1,512,1024]{2,1,0:T(8,128)} fusion(bf16[512,512]{1,0:T(8,128)(2,1)S(1)} %get-tuple-element.7, bf16[512,1024]{1,0:T(8,128)(2,1)S(1)} %get-tuple-element.8), kind=kOutput, calls=%fused_computation | convolution fusion | flops 536870912 | bytes 3670016 | tf_op jit(solution)/shard_map/dot_general | solution.py:320
Async XLA Ops:
  0.7 1.0 %copy-start = (bf16[1,256,1024]{2,1,0:T(8,128)(2,1)S(1)}, bf16[1,256,1024]{2,1,0:T(8,128)(2,1)}, u32[]{:S(2)}) copy-start(bf16[1,256,1024]{2,1,0:T(8,128)(2,1)} %param.8) | copy-start | bytes 1572868
  1.8 0.9 %copy-start.1 = (bf16[1,1,128,1024]{3,2,1,0:T(8,128)(2,1)S(1)}, bf16[1,1,128,1024]{3,2,1,0:T(8,128)(2,1)}, u32[]{:S(2)}) copy-start(bf16[1,1,128,1024]{3,2,1,0:T(8,128)(2,1)} %param.7) | copy-start | bytes 786436
  2.7 0.7 %copy-start.2 = (f32[1,1024]{1,0:T(1,128)S(1)}, f32[1,1024]{1,0:T(1,128)}, u32[]{:S(2)}) copy-start(f32[1,1024]{1,0:T(1,128)} %center_ref.1) | copy-start | bytes 12292
  3.4 0.7 %copy-start.3 = (f32[1,1024]{1,0:T(1,128)S(1)}, f32[1,1024]{1,0:T(1,128)}, u32[]{:S(2)}) copy-start(f32[1,1024]{1,0:T(1,128)} %spread_ref.1) | copy-start | bytes 12292
  4.1 0.7 %copy-start.4 = (f32[1,1024]{1,0:T(1,128)S(1)}, f32[1,1024]{1,0:T(1,128)}, u32[]{:S(2)}) copy-start(f32[1,1024]{1,0:T(1,128)} %gain_ref.1) | copy-start | bytes 12292
  4.8 0.7 %copy-start.5 = (f32[1,64]{1,0:T(1,128)S(1)}, f32[1,64]{1,0:T(1,128)}, u32[]{:S(2)}) copy-start(f32[1,64]{1,0:T(1,128)} %shift_ref.1) | copy-start | bytes 772

commit v2 on v1

v2 whole, which is shorter than its diff:
```python
import functools

import jax
import jax.numpy as jnp
from jax import lax
from jax.experimental import pallas as pl
from jax.experimental.pallas import tpu as pltpu
from jax.sharding import PartitionSpec as P

MESH = pl.DeviceIdType.MESH
F32 = jnp.float32
BF16 = jnp.bfloat16


def log2(n):
    assert n & (n - 1) == 0
    return n.bit_length() - 1


def iota(shape, dim):
    return lax.broadcasted_iota(jnp.int32, shape, dim)


def keep(mask, value):
    return jnp.where(mask, value, jnp.zeros_like(value))


def kernel(
    nz, na, subs, cap,
    x_hbm, w_ref, targets_hbm, shift_hbm, center_hbm, spread_hbm, gain_hbm,
    g_out, tile_out,
    x_ref, targets_ref, shift_ref, center_ref, spread_ref, gain_ref,
    w_full, send_rows, rows, w_proj, g_recv, meta, pos,
    in_sem, own_sem, row_ss, row_rs, up_ss, down_ss, wz_rs, wy_ss, wy_rs, wc_ss, wc_rs,
    wd_ss, wd_rs, meta_ss, meta_rs, g_ss, g_rs,
):
    p = lax.axis_index("parts")
    z = lax.axis_index("slab")
    a = lax.axis_index("ang")
    c = lax.axis_index("chan")
    inputs = [
        pltpu.make_async_copy(src, dst, in_sem.at[i])
        for i, (src, dst) in enumerate((
            (targets_hbm, targets_ref), (shift_hbm, shift_ref), (center_hbm, center_ref),
            (spread_hbm, spread_ref), (gain_hbm, gain_ref), (x_hbm, x_ref),
        ))
    ]
    for copy in inputs:
        copy.start()
    v_rows, width = x_ref.shape
    x_block = w_ref.shape[0]
    quarter = x_block // 4
    sub_rows = v_rows // subs
    total = nz * subs
    piece = cap * sub_rows
    slots = nz * piece
    x_part = g_out.shape[0]
    l_sub, l_subs, l_piece = log2(sub_rows), log2(subs), log2(piece)

    barrier = pltpu.get_barrier_semaphore()
    for d in range(1, nz):
        pl.semaphore_signal(
            barrier, inc=1, device_id={"slab": lax.rem(z + d, nz)}, device_id_type=MESH
        )
    for d in range(1, na):
        pl.semaphore_signal(
            barrier, inc=1, device_id={"ang": lax.rem(a + d, na)}, device_id_type=MESH
        )
    pl.semaphore_signal(barrier, inc=1, device_id={"parts": 1 - p}, device_id_type=MESH)
    pl.semaphore_signal(barrier, inc=1, device_id={"chan": 1 - c}, device_id_type=MESH)

    pl.semaphore_wait(barrier, nz - 1 + na - 1 + 2)

    def weight_slice(s, qp, qc):
        start = pl.multiple_of(s * x_block + (qp * 2 + qc) * quarter, quarter)
        return w_full.at[pl.ds(start, quarter)]

    def weight_copy(s, qp, qc, ss, rs, device, src=None):
        block = weight_slice(s, qp, qc)
        return pltpu.make_async_remote_copy(
            src_ref=block if src is None else src, dst_ref=block,
            send_sem=ss.at[s], recv_sem=rs.at[s], device_id=device, device_id_type=MESH,
        )

    def up(s, src=None):
        return weight_copy(s, p, c, up_ss, wz_rs, {"slab": lax.rem(z + 1, nz)}, src)

    def down(s, src=None):
        return weight_copy(s, p, c, down_ss, wz_rs, {"slab": lax.rem(z + nz - 1, nz)}, src)

    def across(s, qp=p):
        return weight_copy(s, qp, c, wy_ss, wy_rs, {"parts": 1 - p})

    def twin(s, qc=c):
        return weight_copy(s, p, qc, wc_ss, wc_rs, {"chan": 1 - c})

    def twin_far(s, qc=c):
        return weight_copy(s, 1 - p, qc, wd_ss, wd_rs, {"chan": 1 - c})

    own_quarter = w_ref.at[pl.ds(pl.multiple_of((p * 2 + c) * quarter, quarter), quarter)]

    @pl.when(z + 1 < nz)
    def _():
        up(z, own_quarter).start()

    @pl.when(z > 0)
    def _():
        down(z, own_quarter).start()

    own_copy = pltpu.make_async_copy(
        w_ref, w_full.at[pl.ds(pl.multiple_of(z * x_block, x_block), x_block)], own_sem
    )
    own_copy.start()

    for copy in inputs[:-1]:
        copy.wait()
    t_row = targets_ref[...].astype(F32)
    eye = iota((total, total), 0) == iota((total, total), 1)
    t_col = jnp.sum(keep(eye, jnp.broadcast_to(t_row, (total, total))), axis=1, keepdims=True)
    meta[a, 0:1, :] = center_ref[...]
    meta[a, 1:2, :] = spread_ref[...]
    meta[a, 2:3, :] = gain_ref[...]
    meta[a, 3:4, 0:total] = t_row
    meta[a, 4:5, 0:total] = shift_ref[...]

    b_of_v = z * subs + (iota((total, v_rows), 1) >> l_sub)
    b_col = iota((total, v_rows), 0)
    t_wide = jnp.broadcast_to(t_col, (total, v_rows))
    t_v = jnp.sum(keep(b_col == b_of_v, t_wide), axis=0, keepdims=True)
    before = (t_wide == t_v) & (b_col >= z * subs) & (b_col < b_of_v)
    rank_v = jnp.sum(before.astype(F32), axis=0, keepdims=True)
    slot = iota((slots, v_rows), 0)
    v_id = iota((slots, v_rows), 1)
    pick = (
        (t_v == (slot >> l_piece).astype(F32))
        & (rank_v == ((slot & (piece - 1)) >> l_sub).astype(F32))
        & ((v_id & (sub_rows - 1)) == (slot & (sub_rows - 1)))
    )
    inputs[-1].wait()
    send_rows[...] = jnp.dot(
        pick.astype(F32).astype(BF16), x_ref[...], preferred_element_type=F32
    ).astype(BF16)

    def make_tile(src_a):
        t_r = meta[src_a, 3:4, 0:total]
        s_r = meta[src_a, 4:5, 0:total]
        t_c = jnp.sum(keep(eye, jnp.broadcast_to(t_r, (total, total))), axis=1, keepdims=True)
        b0, b1 = iota((total, total), 0), iota((total, total), 1)
        earlier = (t_c == t_r) & ((b0 >> l_subs) == (b1 >> l_subs)) & (b0 < b1)
        rank = jnp.sum(earlier.astype(F32), axis=0, keepdims=True)
        sl = iota((slots, total), 0)
        b = iota((slots, total), 1)
        match = (
            ((b >> l_subs) == (sl >> l_piece))
            & (t_r == z.astype(F32))
            & (rank == ((sl & (piece - 1)) >> l_sub).astype(F32))
        )
        shift = jnp.sum(keep(match, jnp.broadcast_to(s_r, (slots, total))), axis=1, keepdims=True)
        j = (iota((slots, 1), 0) & (sub_rows - 1)).astype(F32)
        pos[...] = j + 0.5 - shift
        center = meta[src_a, 0:1, :]
        spread = meta[src_a, 1:2, :]
        scale = meta[src_a, 2:3, :] * lax.rsqrt(spread)
        inverse = 1.0 / spread
        step = min(32, slots)

        @pl.loop(0, slots // step)
        def _(i):
            at = pl.multiple_of(i * step, step)
            offset = (pos[pl.ds(at, step), :] - center) * inverse
            tile_out[pl.ds(pl.multiple_of(src_a * slots + at, step), step), :] = (
                scale / (1.0 + offset * offset)
            ).astype(BF16)

    def row_copy(src_z, dst_z):
        return pltpu.make_async_remote_copy(
            src_ref=send_rows.at[pl.ds(pl.multiple_of(dst_z * piece, piece), piece)],
            dst_ref=rows.at[pl.ds(pl.multiple_of(src_z * piece, piece), piece)],
            send_sem=row_ss.at[dst_z], recv_sem=row_rs.at[src_z],
            device_id={"slab": dst_z}, device_id_type=MESH,
        )

    row_copy(z, lax.rem(z + nz // 2, nz)).start()

    def meta_copy(src_a, dst_a):
        return pltpu.make_async_remote_copy(
            src_ref=meta.at[src_a], dst_ref=meta.at[src_a],
            send_sem=meta_ss.at[dst_a], recv_sem=meta_rs.at[src_a],
            device_id={"ang": dst_a}, device_id_type=MESH,
        )

    for d in range(1, na):
        meta_copy(a, lax.rem(a + d, na)).start()

    mine = pl.ds(pl.multiple_of(z * piece, piece), piece)
    rows[mine, :] = send_rows[mine, :]

    make_tile(a)
    for d in range(1, na):
        src_a = lax.rem(a + d, na)
        meta_copy(src_a, a).wait_recv()
        make_tile(src_a)


    parts_of = nz // na

    def g_copy(s, src_a, dst_a):
        at = pl.multiple_of(lax.rem(s, parts_of) * x_block, x_block)
        return pltpu.make_async_remote_copy(
            src_ref=w_proj.at[pl.ds(pl.multiple_of(s * x_block, x_block), x_block)],
            dst_ref=g_recv.at[src_a, pl.ds(at, x_block)],
            send_sem=g_ss.at[s], recv_sem=g_rs.at[src_a * parts_of + lax.rem(s, parts_of)],
            device_id={"ang": dst_a}, device_id_type=MESH,
        )

    def project(s):
        at = pl.ds(pl.multiple_of(s * x_block, x_block), x_block)
        block = lax.dot_general(
            w_full[at, :], rows[...], (((1,), (1,)), ((), ())), preferred_element_type=F32
        ).astype(BF16)
        dst_a = s // parts_of

        @pl.when(dst_a != a)
        def _():
            w_proj[at, :] = block
            g_copy(s, a, dst_a).start()

        @pl.when(dst_a == a)
        def _():
            g_recv[
                a, pl.ds(pl.multiple_of(lax.rem(s, parts_of) * x_block, x_block), x_block), :
            ] = block

    pace = [d for d in range(1, nz) if d != nz // 2]
    for t in range(1, nz + 2):
        if t < nz:
            below, above = z - t, z + t

            @pl.when(below >= 0)
            def _():
                up(below).wait_recv()

                @pl.when(z + 1 < nz)
                def _():
                    up(below).start()

                across(below).start()
                twin(below).start()

            @pl.when(above < nz)
            def _():
                down(above).wait_recv()

                @pl.when(z > 0)
                def _():
                    down(above).start()

                across(above).start()
                twin(above).start()

            if t == 1:
                for d in pace:
                    row_copy(z, lax.rem(z + d, nz)).start()
        if 1 < t <= nz:
            for s in (z - t + 1, z + t - 1):
                @pl.when((s >= 0) & (s < nz))
                def _():
                    across(s, 1 - p).wait_recv()
                    twin_far(s).start()
        if t == 2:
            for d in range(1, nz):
                row_copy(lax.rem(z + d, nz), z).wait_recv()
            own_copy.wait()
            project(z)
        if t > 2:
            for s in (z - t + 2, z + t - 2):
                @pl.when((s >= 0) & (s < nz))
                def _():
                    twin(s, 1 - c).wait_recv()
                    twin_far(s, 1 - c).wait_recv()
                    project(s)

    for d in range(1, na):
        src_a = lax.rem(a + d, na)
        for k in range(parts_of):
            g_copy(a * parts_of + k, src_a, a).wait_recv()
    for k in range(na):
        g_out[:, k * slots:(k + 1) * slots] = g_recv[k]

    for d in range(1, nz):
        row_copy(z, lax.rem(z + d, nz)).wait_send()
    for d in range(1, na):
        meta_copy(a, lax.rem(a + d, na)).wait_send()
    for s in range(nz):
        @pl.when(s // parts_of != a)
        def _():
            g_copy(s, a, s // parts_of).wait_send()

        @pl.when((s <= z) & (z + 1 < nz))
        def _():
            up(s).wait_send()

        @pl.when((s >= z) & (z > 0))
        def _():
            down(s).wait_send()

        @pl.when(s != z)
        def _():
            across(s).wait_send()
            twin(s).wait_send()
            twin_far(s).wait_send()


def shards(sinogram, transaxial, targets, row_shift, center, spread, gain):
    nz = lax.axis_size("slab")
    na = lax.axis_size("ang")
    detector = sinogram[0, 0]
    weights = transaxial[0]
    v_rows, width = detector.shape
    total = targets.shape[1]
    subs = total // nz
    sub_rows = v_rows // subs
    cap = max(2, 2 * subs // nz)
    piece = cap * sub_rows
    slots = nz * piece
    x_all = weights.shape[0] * nz
    x_part = x_all // na
    r_rows = center.shape[1]
    vmem = pl.BlockSpec(memory_space=pltpu.VMEM)
    dma = pltpu.SemaphoreType.DMA
    projected, tile = pl.pallas_call(
        functools.partial(kernel, nz, na, subs, cap),
        out_shape=(
            jax.ShapeDtypeStruct((x_part, na * slots), BF16),
            jax.ShapeDtypeStruct((na * slots, r_rows), BF16),
        ),
        in_specs=[pl.BlockSpec(memory_space=pl.ANY)] * 7,
        out_specs=(vmem, vmem),
        scratch_shapes=[
            pltpu.VMEM((v_rows, width), BF16),
            pltpu.VMEM((1, total), jnp.int32),
            pltpu.VMEM((1, total), F32),
            pltpu.VMEM((1, r_rows), F32),
            pltpu.VMEM((1, r_rows), F32),
            pltpu.VMEM((1, r_rows), F32),
            pltpu.VMEM((x_all, width), BF16),
            pltpu.VMEM((slots, width), BF16),
            pltpu.VMEM((slots, width), BF16),
            pltpu.VMEM((x_all, slots), BF16),
            pltpu.VMEM((na, x_part, slots), BF16),
            pltpu.VMEM((na, 8, r_rows), F32),
            pltpu.VMEM((slots, 1), F32),
            dma((6,)),
            dma(()),
        ] + [dma((nz,))] * 11 + [dma((na,))] * 2 + [dma((nz,))] * 2,
        compiler_params=pltpu.CompilerParams(
            collective_id=0, has_side_effects=True, vmem_limit_bytes=60 * 1024 * 1024
        ),
    )(detector, weights, targets[..., 0], row_shift, center, spread, gain)
    volume = jnp.dot(projected, tile, preferred_element_type=F32)
    return volume[None]


def solution(mesh):
    assert mesh.shape["parts"] == 2 and mesh.shape["chan"] == 2
    in_specs = (
        P(("parts", "chan"), "ang", "slab", None),
        P("ang", "slab", None),
        P("ang", None, None),
        P("ang", None),
        P("ang", "slab"),
        P("ang", "slab"),
        P("ang", "slab"),
    )
    out_specs = P(("parts", "chan"), "ang", "slab")
    return jax.shard_map(shards, mesh=mesh, in_specs=in_specs, out_specs=out_specs, check_vma=False)
```

time: 49.2 us -> 40.4 us (0.82)
  local copies, waits for them, and re-layouts: 5.45 us -> 0 us
  Pallas kernels: 41.4 us -> 36.8 us
  matrix products: 2.03 us -> 3.42 us
    unnamed x12 -> x0, local copies, waits for them, and re-layouts: 4.7 us -> none
    pallas_call x1, Pallas kernels: 41.4 us -> 36.8 us  [shards(): pl.pallas_call(functools.partial(kernel, nz, na, subs, cap), out_shape=(j...]
    dot_general x1, matrix products: 2.03 us -> 3.42 us  [shards(): volume = jnp.dot(projected, tile, preferred_element_type=F32)]
    squeeze x1 -> x0, local copies, waits for them, and re-layouts: 0.74 us -> none  [shards(): targets[0]]
where the time goes in v2:
time: 40.4 us; the launch traced here: 40.2 us
  Pallas kernels  36.8 us (91%)
  matrix products  3.42 us (8%)
    pallas_call x1, Pallas kernels, shards(): pl.pallas_call(functools.partial(kernel, nz, na, subs, cap), out_shape=(j...  36.8 us
    dot_general x1, matrix products, shards(): volume = jnp.dot(projected, tile, preferred_element_type=F32)  3.42 us

profile of v2, /device:TPU:0, one launch (start us, length us, event | category | flops | bytes accessed | tf_op | source)
XLA Modules:
  0.0 40.2 jit_solution(17195871811832296120)
XLA Ops:
  0.0 36.8 %shard_map.73 = (bf16[512,512]{1,0:T(8,128)(2,1)}, bf16[512,1024]{1,0:T(8,128)(2,1)}) custom-call(bf16[128,1024]{1,0:T(8,128)(2,1)} %bitcast.8, bf16[256,1024]{1,0:T(8,128)(2,1)} %bitcast.7, s32[1,64]{1,0:T(1,128)} %bitcast.9, f32[1,64]{1,0:T(1,128)} %shift_hbm.1, f32[1,1024]{1,0:T(1,128)} %center_hbm.1, f32[1,1024]{1,0:T(1,128)} %spread_hbm.1, ...), custom_call_target="tpu_custom_call" | custom-call | tf_op jit(solution)/shard_map/pallas_call | solution.py:331
  36.8 3.4 %convolution_bitcast_fusion = f32[1,512,1024]{2,1,0:T(8,128)} fusion(bf16[512,512]{1,0:T(8,128)(2,1)} %get-tuple-element.7, bf16[512,1024]{1,0:T(8,128)(2,1)} %get-tuple-element.8), kind=kOutput, calls=%fused_computation | convolution fusion | flops 536870912 | bytes 3670016 | tf_op jit(solution)/shard_map/dot_general | solution.py:360

commit v3 on v2

--- a/solution.py
+++ b/solution.py
@@ -26,7 +26,7 @@
 
 
 def kernel(
-    nz, na, subs, cap,
+    nz, na, subs, cap, halves,
     x_hbm, w_ref, targets_hbm, shift_hbm, center_hbm, spread_hbm, gain_hbm,
     g_out, tile_out,
     x_ref, targets_ref, shift_ref, center_ref, spread_ref, gain_ref,
@@ -49,7 +49,8 @@
         copy.start()
     v_rows, width = x_ref.shape
     x_block = w_ref.shape[0]
-    quarter = x_block // 4
+    x_half = x_block // halves
+    grain = x_half // 4
     sub_rows = v_rows // subs
     total = nz * subs
     piece = cap * sub_rows
@@ -71,41 +72,41 @@
 
     pl.semaphore_wait(barrier, nz - 1 + na - 1 + 2)
 
-    def weight_slice(s, qp, qc):
-        start = pl.multiple_of(s * x_block + (qp * 2 + qc) * quarter, quarter)
-        return w_full.at[pl.ds(start, quarter)]
-
-    def weight_copy(s, qp, qc, ss, rs, device, src=None):
-        block = weight_slice(s, qp, qc)
+    def weight_copy(s, h, qp, qc, ss, rs, device, src=None):
+        start = s * x_block + h * x_half + (qp * 2 + qc) * grain
+        block = w_full.at[pl.ds(pl.multiple_of(start, grain), grain)]
         return pltpu.make_async_remote_copy(
             src_ref=block if src is None else src, dst_ref=block,
-            send_sem=ss.at[s], recv_sem=rs.at[s], device_id=device, device_id_type=MESH,
-        )
-
-    def up(s, src=None):
-        return weight_copy(s, p, c, up_ss, wz_rs, {"slab": lax.rem(z + 1, nz)}, src)
-
-    def down(s, src=None):
-        return weight_copy(s, p, c, down_ss, wz_rs, {"slab": lax.rem(z + nz - 1, nz)}, src)
-
-    def across(s, qp=p):
-        return weight_copy(s, qp, c, wy_ss, wy_rs, {"parts": 1 - p})
-
-    def twin(s, qc=c):
-        return weight_copy(s, p, qc, wc_ss, wc_rs, {"chan": 1 - c})
-
-    def twin_far(s, qc=c):
-        return weight_copy(s, 1 - p, qc, wd_ss, wd_rs, {"chan": 1 - c})
-
-    own_quarter = w_ref.at[pl.ds(pl.multiple_of((p * 2 + c) * quarter, quarter), quarter)]
-
-    @pl.when(z + 1 < nz)
-    def _():
-        up(z, own_quarter).start()
-
-    @pl.when(z > 0)
-    def _():
-        down(z, own_quarter).start()
+            send_sem=ss.at[s * halves + h], recv_sem=rs.at[s * halves + h],
+            device_id=device, device_id_type=MESH,
+        )
+
+    def up(s, h, src=None):
+        return weight_copy(s, h, p, c, up_ss, wz_rs, {"slab": lax.rem(z + 1, nz)}, src)
+
+    def down(s, h, src=None):
+        return weight_copy(s, h, p, c, down_ss, wz_rs, {"slab": lax.rem(z + nz - 1, nz)}, src)
+
+    def across(s, h, qp=p):
+        return weight_copy(s, h, qp, c, wy_ss, wy_rs, {"parts": 1 - p})
+
+    def twin(s, h, qc=c):
+        return weight_copy(s, h, p, qc, wc_ss, wc_rs, {"chan": 1 - c})
+
+    def twin_far(s, h, qc=c):
+        return weight_copy(s, h, 1 - p, qc, wd_ss, wd_rs, {"chan": 1 - c})
+
+    for h in range(halves):
+        start = h * x_half + (p * 2 + c) * grain
+        own = w_ref.at[pl.ds(pl.multiple_of(start, grain), grain)]
+
+        @pl.when(z + 1 < nz)
+        def _():
+            up(z, h, own).start()
+
+        @pl.when(z > 0)
+        def _():
+            down(z, h, own).start()
 
     own_copy = pltpu.make_async_copy(
         w_ref, w_full.at[pl.ds(pl.multiple_of(z * x_block, x_block), x_block)], own_sem
@@ -204,17 +205,19 @@
 
     parts_of = nz // na
 
-    def g_copy(s, src_a, dst_a):
-        at = pl.multiple_of(lax.rem(s, parts_of) * x_block, x_block)
+    def g_copy(s, h, src_a, dst_a):
+        near = lax.rem(s, parts_of)
+        at = pl.multiple_of(near * x_block + h * x_half, x_half)
         return pltpu.make_async_remote_copy(
-            src_ref=w_proj.at[pl.ds(pl.multiple_of(s * x_block, x_block), x_block)],
-            dst_ref=g_recv.at[src_a, pl.ds(at, x_block)],
-            send_sem=g_ss.at[s], recv_sem=g_rs.at[src_a * parts_of + lax.rem(s, parts_of)],
+            src_ref=w_proj.at[pl.ds(pl.multiple_of(s * x_block + h * x_half, x_half), x_half)],
+            dst_ref=g_recv.at[src_a, pl.ds(at, x_half)],
+            send_sem=g_ss.at[s * halves + h],
+            recv_sem=g_rs.at[(src_a * parts_of + near) * halves + h],
             device_id={"ang": dst_a}, device_id_type=MESH,
         )
 
-    def project(s):
-        at = pl.ds(pl.multiple_of(s * x_block, x_block), x_block)
+    def project(s, h):
+        at = pl.ds(pl.multiple_of(s * x_block + h * x_half, x_half), x_half)
         block = lax.dot_general(
             w_full[at, :], rows[...], (((1,), (1,)), ((), ())), preferred_element_type=F32
         ).astype(BF16)
@@ -223,67 +226,83 @@
         @pl.when(dst_a != a)
         def _():
             w_proj[at, :] = block
-            g_copy(s, a, dst_a).start()
+            g_copy(s, h, a, dst_a).start()
 
         @pl.when(dst_a == a)
         def _():
-            g_recv[
-                a, pl.ds(pl.multiple_of(lax.rem(s, parts_of) * x_block, x_block), x_block), :
-            ] = block
-
-    pace = [d for d in range(1, nz) if d != nz // 2]
-    for t in range(1, nz + 2):
-        if t < nz:
-            below, above = z - t, z + t
-
-            @pl.when(below >= 0)
-            def _():
-                up(below).wait_recv()
-
-                @pl.when(z + 1 < nz)
-                def _():
-                    up(below).start()
-
-                across(below).start()
-                twin(below).start()
-
-            @pl.when(above < nz)
-            def _():
-                down(above).wait_recv()
-
-                @pl.when(z > 0)
-                def _():
-                    down(above).start()
-
-                across(above).start()
-                twin(above).start()
-
-            if t == 1:
-                for d in pace:
-                    row_copy(z, lax.rem(z + d, nz)).start()
-        if 1 < t <= nz:
-            for s in (z - t + 1, z + t - 1):
-                @pl.when((s >= 0) & (s < nz))
-                def _():
-                    across(s, 1 - p).wait_recv()
-                    twin_far(s).start()
-        if t == 2:
+            here = lax.rem(s, parts_of) * x_block + h * x_half
+            g_recv[a, pl.ds(pl.multiple_of(here, x_half), x_half), :] = block
+
+    pace = [d for d in range(nz - 1, 0, -1) if d != nz // 2]
+    def pass_on(t, h):
+        below, above = z - t, z + t
+
+        @pl.when(below >= 0)
+        def _():
+            up(below, h).wait_recv()
+
+            @pl.when(z + 1 < nz)
+            def _():
+                up(below, h).start()
+
+            across(below, h).start()
+            twin(below, h).start()
+
+        @pl.when(above < nz)
+        def _():
+            down(above, h).wait_recv()
+
+            @pl.when(z > 0)
+            def _():
+                down(above, h).start()
+
+            across(above, h).start()
+            twin(above, h).start()
+
+    def pass_to_twin(t, h):
+        for s in (z - t, z + t):
+            @pl.when((s >= 0) & (s < nz))
+            def _():
+                across(s, h, 1 - p).wait_recv()
+                twin_far(s, h).start()
+
+    def finish(t, h):
+        for s in (z - t, z + t):
+            @pl.when((s >= 0) & (s < nz))
+            def _():
+                twin(s, h, 1 - c).wait_recv()
+                twin_far(s, h, 1 - c).wait_recv()
+                project(s, h)
+
+    steps = [(t, h) for t in range(1, nz) for h in range(halves)]
+    ready = 2 * halves - 1
+    done = 0
+    for i, step in enumerate(steps):
+        pass_on(*step)
+        if i == halves - 1:
+            for d in pace:
+                row_copy(z, lax.rem(z + d, nz)).start()
+        if i:
+            pass_to_twin(*steps[i - 1])
+        if i == ready:
             for d in range(1, nz):
                 row_copy(lax.rem(z + d, nz), z).wait_recv()
             own_copy.wait()
-            project(z)
-        if t > 2:
-            for s in (z - t + 2, z + t - 2):
-                @pl.when((s >= 0) & (s < nz))
-                def _():
-                    twin(s, 1 - c).wait_recv()
-                    twin_far(s, 1 - c).wait_recv()
-                    project(s)
+            for h in range(halves):
+                project(z, h)
+        if i >= ready:
+            while done < i - 1:
+                finish(*steps[done])
+                done += 1
+    pass_to_twin(*steps[-1])
+    for step in steps[done:]:
+        finish(*step)
 
     for d in range(1, na):
         src_a = lax.rem(a + d, na)
         for k in range(parts_of):
-            g_copy(a * parts_of + k, src_a, a).wait_recv()
+            for h in range(halves):
+                g_copy(a * parts_of + k, h, src_a, a).wait_recv()
     for k in range(na):
         g_out[:, k * slots:(k + 1) * slots] = g_recv[k]
 
@@ -294,21 +313,23 @@
     for s in range(nz):
         @pl.when(s // parts_of != a)
         def _():
-            g_copy(s, a, s // parts_of).wait_send()
-
-        @pl.when((s <= z) & (z + 1 < nz))
-        def _():
-            up(s).wait_send()
-
-        @pl.when((s >= z) & (z > 0))
-        def _():
-            down(s).wait_send()
-
-        @pl.when(s != z)
-        def _():
-            across(s).wait_send()
-            twin(s).wait_send()
-            twin_far(s).wait_send()
+            for h in range(halves):
+                g_copy(s, h, a, s // parts_of).wait_send()
+
+        for h in range(halves):
+            @pl.when((s <= z) & (z + 1 < nz))
+            def _():
+                up(s, h).wait_send()
+
+            @pl.when((s >= z) & (z > 0))
+            def _():
+                down(s, h).wait_send()
+
+            @pl.when(s != z)
+            def _():
+                across(s, h).wait_send()
+                twin(s, h).wait_send()
+                twin_far(s, h).wait_send()
 
 
 def shards(sinogram, transaxial, targets, row_shift, center, spread, gain):
@@ -326,10 +347,11 @@
     x_all = weights.shape[0] * nz
     x_part = x_all // na
     r_rows = center.shape[1]
+    halves = max(1, min(2, weights.shape[0] // 4 // 16))
     vmem = pl.BlockSpec(memory_space=pltpu.VMEM)
     dma = pltpu.SemaphoreType.DMA
     projected, tile = pl.pallas_call(
-        functools.partial(kernel, nz, na, subs, cap),
+        functools.partial(kernel, nz, na, subs, cap, halves),
         out_shape=(
             jax.ShapeDtypeStruct((x_part, na * slots), BF16),
             jax.ShapeDtypeStruct((na * slots, r_rows), BF16),
@@ -352,7 +374,7 @@
             pltpu.VMEM((slots, 1), F32),
             dma((6,)),
             dma(()),
-        ] + [dma((nz,))] * 11 + [dma((na,))] * 2 + [dma((nz,))] * 2,
+        ] + [dma((nz,))] * 2 + [dma((nz * halves,))] * 9 + [dma((na,))] * 2 + [dma((nz * halves,))] * 2,
         compiler_params=pltpu.CompilerParams(
             collective_id=0, has_side_effects=True, vmem_limit_bytes=60 * 1024 * 1024
         ),

time: 40.4 us -> 38.1 us (0.943)
  Pallas kernels: 36.8 us -> 34.5 us
    pallas_call x1, Pallas kernels: 36.8 us -> 34.5 us  [shards(): pl.pallas_call(functools.partial(kernel, nz, na, subs, cap, halves), out_...]
where the time goes in v3:
time: 38.1 us; the launch traced here: 37.9 us
  Pallas kernels  34.5 us (91%)
  matrix products  3.42 us (9%)
    pallas_call x1, Pallas kernels, shards(): pl.pallas_call(functools.partial(kernel, nz, na, subs, cap, halves), out_...  34.5 us
    dot_general x1, matrix products, shards(): volume = jnp.dot(projected, tile, preferred_element_type=F32)  3.42 us

profile of v3, /device:TPU:0, one launch (start us, length us, event | category | flops | bytes accessed | tf_op | source)
XLA Modules:
  0.0 37.9 jit_solution(16521496676187827222)
XLA Ops:
  0.0 34.5 %shard_map.73 = (bf16[512,512]{1,0:T(8,128)(2,1)}, bf16[512,1024]{1,0:T(8,128)(2,1)}) custom-call(bf16[128,1024]{1,0:T(8,128)(2,1)} %bitcast.8, bf16[256,1024]{1,0:T(8,128)(2,1)} %bitcast.7, s32[1,64]{1,0:T(1,128)} %bitcast.9, f32[1,64]{1,0:T(1,128)} %shift_hbm.1, f32[1,1024]{1,0:T(1,128)} %center_hbm.1, f32[1,1024]{1,0:T(1,128)} %spread_hbm.1, ...), custom_call_target="tpu_custom_call" | custom-call | tf_op jit(solution)/shard_map/pallas_call | solution.py:353
  34.5 3.4 %convolution_bitcast_fusion = f32[1,512,1024]{2,1,0:T(8,128)} fusion(bf16[512,512]{1,0:T(8,128)(2,1)} %get-tuple-element.7, bf16[512,1024]{1,0:T(8,128)(2,1)} %get-tuple-element.8), kind=kOutput, calls=%fused_computation | convolution fusion | flops 536870912 | bytes 3670016 | tf_op jit(solution)/shard_map/dot_general | solution.py:382

commit v4 on v3

--- a/solution.py
+++ b/solution.py
@@ -196,12 +196,6 @@
     mine = pl.ds(pl.multiple_of(z * piece, piece), piece)
     rows[mine, :] = send_rows[mine, :]
 
-    make_tile(a)
-    for d in range(1, na):
-        src_a = lax.rem(a + d, na)
-        meta_copy(src_a, a).wait_recv()
-        make_tile(src_a)
-
 
     parts_of = nz // na
 
@@ -284,6 +278,13 @@
                 row_copy(z, lax.rem(z + d, nz)).start()
         if i:
             pass_to_twin(*steps[i - 1])
+        if i == halves - 1:
+            make_tile(a)
+        if i == halves:
+            for d in range(1, na):
+                src_a = lax.rem(a + d, na)
+                meta_copy(src_a, a).wait_recv()
+                make_tile(src_a)
         if i == ready:
             for d in range(1, nz):
                 row_copy(lax.rem(z + d, nz), z).wait_recv()

time: 38.1 us -> 37.2 us (0.976)
  Pallas kernels: 34.5 us -> 33.7 us
    pallas_call x1, Pallas kernels: 34.5 us -> 33.7 us  [shards(): pl.pallas_call(functools.partial(kernel, nz, na, subs, cap, halves), out_...]
where the time goes in v4:
time: 37.2 us; the launch traced here: 37.1 us
  Pallas kernels  33.7 us (91%)
  matrix products  3.42 us (9%)
    pallas_call x1, Pallas kernels, shards(): pl.pallas_call(functools.partial(kernel, nz, na, subs, cap, halves), out_...  33.7 us
    dot_general x1, matrix products, shards(): volume = jnp.dot(projected, tile, preferred_element_type=F32)  3.42 us

profile of v4, /device:TPU:0, one launch (start us, length us, event | category | flops | bytes accessed | tf_op | source)
XLA Modules:
  0.0 37.1 jit_solution(8432320540974173491)
XLA Ops:
  0.0 33.7 %shard_map.73 = (bf16[512,512]{1,0:T(8,128)(2,1)}, bf16[512,1024]{1,0:T(8,128)(2,1)}) custom-call(bf16[128,1024]{1,0:T(8,128)(2,1)} %bitcast.8, bf16[256,1024]{1,0:T(8,128)(2,1)} %bitcast.7, s32[1,64]{1,0:T(1,128)} %bitcast.9, f32[1,64]{1,0:T(1,128)} %shift_hbm.1, f32[1,1024]{1,0:T(1,128)} %center_hbm.1, f32[1,1024]{1,0:T(1,128)} %spread_hbm.1, ...), custom_call_target="tpu_custom_call" | custom-call | tf_op jit(solution)/shard_map/pallas_call | solution.py:354
  33.7 3.4 %convolution_bitcast_fusion = f32[1,512,1024]{2,1,0:T(8,128)} fusion(bf16[512,512]{1,0:T(8,128)(2,1)} %get-tuple-element.7, bf16[512,1024]{1,0:T(8,128)(2,1)} %get-tuple-element.8), kind=kOutput, calls=%fused_computation | convolution fusion | flops 536870912 | bytes 3670016 | tf_op jit(solution)/shard_map/dot_general | solution.py:383

commit v5 on v4

--- a/solution.py
+++ b/solution.py
@@ -299,13 +299,13 @@
     for step in steps[done:]:
         finish(*step)
 
+    g_out[:, pl.ds(pl.multiple_of(a * slots, slots), slots)] = g_recv[a]
     for d in range(1, na):
         src_a = lax.rem(a + d, na)
         for k in range(parts_of):
             for h in range(halves):
                 g_copy(a * parts_of + k, h, src_a, a).wait_recv()
-    for k in range(na):
-        g_out[:, k * slots:(k + 1) * slots] = g_recv[k]
+        g_out[:, pl.ds(pl.multiple_of(src_a * slots, slots), slots)] = g_recv[src_a]
 
     for d in range(1, nz):
         row_copy(z, lax.rem(z + d, nz)).wait_send()

time: 37.2 us -> 37.2 us (level)
  no operation moved by 1% of the time
where the time goes in v5:
time: 37.2 us; the launch traced here: 37.1 us
  Pallas kernels  33.7 us (91%)
  matrix products  3.42 us (9%)
    pallas_call x1, Pallas kernels, shards(): pl.pallas_call(functools.partial(kernel, nz, na, subs, cap, halves), out_...  33.7 us
    dot_general x1, matrix products, shards(): volume = jnp.dot(projected, tile, preferred_element_type=F32)  3.42 us

profile of v5, /device:TPU:0, one launch (start us, length us, event | category | flops | bytes accessed | tf_op | source)
XLA Modules:
  0.0 37.1 jit_solution(2593081448084062655)
XLA Ops:
  0.0 33.7 %shard_map.73 = (bf16[512,512]{1,0:T(8,128)(2,1)}, bf16[512,1024]{1,0:T(8,128)(2,1)}) custom-call(bf16[128,1024]{1,0:T(8,128)(2,1)} %bitcast.8, bf16[256,1024]{1,0:T(8,128)(2,1)} %bitcast.7, s32[1,64]{1,0:T(1,128)} %bitcast.9, f32[1,64]{1,0:T(1,128)} %shift_hbm.1, f32[1,1024]{1,0:T(1,128)} %center_hbm.1, f32[1,1024]{1,0:T(1,128)} %spread_hbm.1, ...), custom_call_target="tpu_custom_call" | custom-call | tf_op jit(solution)/shard_map/pallas_call | solution.py:354
  33.7 3.4 %convolution_bitcast_fusion = f32[1,512,1024]{2,1,0:T(8,128)} fusion(bf16[512,512]{1,0:T(8,128)(2,1)} %get-tuple-element.7, bf16[512,1024]{1,0:T(8,128)(2,1)} %get-tuple-element.8), kind=kOutput, calls=%fused_computation | convolution fusion | flops 536870912 | bytes 3670016 | tf_op jit(solution)/shard_map/dot_general | solution.py:383
